TPU v7x, 32 devices: a whole 2x2x4 slice. The times are simulated.
32 devices in a mesh: xy: 2 (over core), gz: 16 (over z, y, x).
Axes of the slice: x: 2, y: 2, z: 4, core: 2. Of those that a mesh axis runs over, the one named last changes fastest.
Arguments:
- volume: bfloat16 [4, 128, 128, 128], P('xy', None, 'gz'), may hold values from -6 to 6
- conv_first: bfloat16 [3, 3, 128, 128], replicated, may hold values from -0.1875 to 0.1875
- conv_second: bfloat16 [3, 3, 128, 128], replicated, may hold values from -0.1875 to 0.1875
- w_qkv: bfloat16 [128, 384], replicated
- w_out: bfloat16 [128, 128], replicated, may hold values from -0.5 to 0.5
Outputs:
- refined: bfloat16 [4, 128, 128, 128], P('xy', None, 'gz')
All inputs are finite; a program needn't handle non-finite values.
Results may differ from a plain program's by a relative error of at most 0.0085.
Values may be sent and summed in bfloat16 or wider, within the bound.
A program may use at most 64 MiB of HBM per device.

v0:
```python
import jax
import jax.numpy as jnp
from jax import lax
from jax.sharding import PartitionSpec as P

HEADS = 4


def padded_2(block, sides, width):
    for axis, dim in sides:
        count = lax.axis_size(axis)
        forward = [(i, i + 1) for i in range(count - 1)]
        backward = [(target, source) for source, target in forward]
        low = lax.ppermute(
            lax.slice_in_dim(block, block.shape[dim] - width, None, axis=dim), axis, forward
        )
        high = lax.ppermute(lax.slice_in_dim(block, 0, width, axis=dim), axis, backward)
        block = jnp.concatenate([low, block, high], axis=dim)
    return block


def conv_local(padded, weight, count):
    cols = padded.shape[1]
    wider = jnp.pad(padded, ((0, 0), (1, 1), (0, 0), (0, 0)))
    total = jnp.zeros((count,) + padded.shape[1:], jnp.float32)
    for shift_r in range(3):
        for shift_c in range(3):
            total = total + jnp.dot(
                wider[shift_r : shift_r + count, shift_c : shift_c + cols],
                weight[shift_r, shift_c],
                preferred_element_type=jnp.float32,
            )
    return total


def project(row, w_qkv):
    values = row.astype(jnp.float32)
    normed = values / jnp.sqrt(jnp.mean(values * values, axis=-1, keepdims=True) + 1e-06)
    return jnp.dot(normed, w_qkv.astype(jnp.float32), preferred_element_type=jnp.float32).astype(
        jnp.bfloat16
    )


def attend(qkv, w_out):
    cols, depth, triple = qkv.shape
    width = triple // 3
    split = qkv.reshape(cols, depth, 3, HEADS, width // HEADS)
    scores = jnp.einsum(
        "cqhd,ckhd->chqk", split[:, :, 0], split[:, :, 1], preferred_element_type=jnp.float32
    )
    scores = scores / jnp.sqrt(jnp.float32(width // HEADS))
    probs = jax.nn.softmax(scores, axis=-1).astype(jnp.bfloat16)
    context = jnp.einsum(
        "chqk,ckhd->cqhd", probs, split[:, :, 2], preferred_element_type=jnp.float32
    ).astype(jnp.bfloat16)
    return jnp.dot(
        context.reshape(cols, depth, width), w_out, preferred_element_type=jnp.float32
    ).astype(jnp.bfloat16)


def on_device(volume, conv_first, conv_second, w_qkv, w_out):
    count = volume.shape[0]
    padded = padded_2(volume, (("xy", 0),), 2)
    hidden = jax.nn.silu(conv_local(padded, conv_first, count + 2)).astype(jnp.bfloat16)
    position = lax.axis_index("xy") * count - 1 + jnp.arange(count + 2, dtype=jnp.int32)
    inside = (position >= 0) & (position < count * lax.axis_size("xy"))
    hidden = jnp.where(inside[:, None, None, None], hidden, jnp.zeros_like(hidden))
    second = conv_local(hidden, conv_second, count)
    mixed = (volume.astype(jnp.float32) + second).astype(jnp.bfloat16)
    attended = lax.map(
        lambda row: attend(project(row, w_qkv), w_out),
        lax.all_to_all(mixed, "gz", split_axis=1, concat_axis=2, tiled=True),
    )
    returned = lax.all_to_all(attended, "gz", split_axis=2, concat_axis=1, tiled=True)
    return (mixed.astype(jnp.float32) + returned.astype(jnp.float32)).astype(jnp.bfloat16)


def solution(mesh):
    placed = (P("xy", None, "gz", None), P(), P(), P(), P())
    return jax.shard_map(
        on_device, mesh=mesh, in_specs=placed, out_specs=P("xy", None, "gz", None), check_vma=False
    )
```

profile of v0, /device:TPU:0, one launch (start us, length us, event | category | flops | bytes accessed | tf_op | source)
XLA Modules:
  0.0 70.5 jit_solution(2601241355634052545)
XLA Ops:
  0.0 1.2 %copy.41 = bf16[2,128,8,128]{3,1,2,0:T(8,128)(2,1)S(1)} copy(bf16[2,128,8,128]{3,2,1,0:T(8,128)(2,1)} %param.7) | data formatting | bytes 1048576 | tf_op args[0]
  1.2 2.4 %collective-permute-start = (bf16[2,128,8,128]{3,1,2,0:T(8,128)(2,1)S(1)}, bf16[2,128,8,128]{3,1,2,0:T(8,128)(2,1)S(1)}, u32[]{:S(2)}, u32[]{:S(2)}) collective-permute-start(bf16[2,128,8,128]{3,1,2,0:T(8,128)(2,1)S(1)} %copy.41), channel_id=1, source_target_pairs={{0,16},{1,17},{2,18},{3,19},{4,20},{5,21},{6,22},{7,23},{8,24},{9,... | collective-permute-start | bytes 1572872 | tf_op jit(solution)/shard_map/ppermute | solution.py:14
  3.6 1.3 %collective-permute-start.1 = (bf16[2,128,8,128]{3,1,2,0:T(8,128)(2,1)S(1)}, bf16[2,128,8,128]{3,1,2,0:T(8,128)(2,1)S(1)}, u32[]{:S(2)}, u32[]{:S(2)}) collective-permute-start(bf16[2,128,8,128]{3,1,2,0:T(8,128)(2,1)S(1)} %copy.41), channel_id=1, source_target_pairs={{16,0},{17,1},{18,2},{19,3},{20,4},{21,5},{22,6},{23,7},{24,8},{25... | collective-permute-start | bytes 1572872 | tf_op jit(solution)/shard_map/ppermute | solution.py:17
  4.9 0.2 collective-permute-done
  5.1 0.1 constant_dynamic-update-slice_fusion.1
  5.3 2.1 %collective-permute-done.1 = bf16[2,128,8,128]{3,1,2,0:T(8,128)(2,1)S(1)} collective-permute-done((bf16[2,128,8,128]{3,1,2,0:T(8,128)(2,1)S(1)}, bf16[2,128,8,128]{3,1,2,0:T(8,128)(2,1)S(1)}, u32[]{:S(2)}, u32[]{:S(2)}) %collective-permute-start.1) | collective-permute-done | bytes 524320 | tf_op jit(solution)/shard_map/ppermute | solution.py:17
  7.4 0.1 constant_dynamic-update-slice_fusion
  7.5 0.4 fusion.36
  7.9 0.4 fusion.38
  8.4 0.4 fusion.40
  8.8 0.4 fusion.42
  9.3 0.4 fusion.44
  9.7 0.4 fusion.71
  10.1 0.4 fusion.20
  10.6 0.4 fusion.24
  11.0 0.0 copy-start.3
  11.0 1.4 %fusion.33 = bf16[4,128,8,128]{3,1,2,0:T(8,128)(2,1)S(1)} fusion(f32[4,128,8,128]{3,1,2,0:T(8,128)S(1)} %fusion.24, f32[4,128,8,128]{3,1,2,0:T(8,128)S(1)} %fusion.36, f32[4,128,8,128]{3,1,2,0:T(8,128)S(1)} %fusion.38, f32[4,128,8,128]{3,1,2,0:T(8,128)S(1)} %fusion.71, f32[4,128,8,128]{3,1,2,0:T(8,128)S(1)} %fusion.40, f32[4,128,8,128]{3,1,2,0:T(8,128)S(1)} %fusion.42, ...), kind=kOutput, calls=%fused_computation.49 | convolution fusion | flops 141557760 | bytes 19431936 | tf_op jit(solution)/shard_map/dot_general | solution.py:28
  12.4 0.3 fusion.52
  12.7 0.3 fusion.53
  13.0 0.3 fusion.54
  13.3 0.3 fusion.55
  13.6 0.3 fusion.56
  13.9 0.3 fusion.57
  14.2 0.3 fusion.18
  14.5 0.3 fusion.16
  14.8 0.3 fusion.19
  15.1 1.1 %copy.47 = bf16[2,128,8,128]{3,2,0,1:T(8,128)(2,1)} copy(bf16[2,128,8,128]{3,1,2,0:T(8,128)(2,1)S(1)} %fusion.19) | data formatting | bytes 1048576 | tf_op jit(solution)/shard_map/convert_element_type | solution.py:69
  16.3 7.7 %all-to-all-start = ((bf16[2,128,8,128]{3,2,0,1:T(8,128)(2,1)}), bf16[2,128,8,128]{3,2,0,1:T(8,128)(2,1)S(1)}, u32[]{:S(2)}, u32[]{:S(2)}) async-start(bf16[2,128,8,128]{3,2,0,1:T(8,128)(2,1)} %copy.47), calls=%async_computation | async-start | bytes 1048576 | tf_op jit(solution)/shard_map/all_to_all | solution.py:72
  24.0 15.4 %all-to-all-done = bf16[2,128,8,128]{3,2,0,1:T(8,128)(2,1)S(1)} async-done(((bf16[2,128,8,128]{3,2,0,1:T(8,128)(2,1)}), bf16[2,128,8,128]{3,2,0,1:T(8,128)(2,1)S(1)}, u32[]{:S(2)}, u32[]{:S(2)}) %all-to-all-start) | async-done | bytes 524320 | tf_op jit(solution)/shard_map/all_to_all | solution.py:72
  39.4 0.1 copy.84
  39.5 11.5 %while.10 = (s32[]{:T(128)}, bf16[2,8,128,128]{3,1,0,2:T(8,128)(2,1)S(1)}, bf16[2,8,128,128]{3,2,1,0:T(8,128)(2,1)S(1)}, bf16[128,384]{1,0:T(8,128)(2,1)S(1)}, bf16[128,128]{1,0:T(8,128)(2,1)S(1)}, /*index=5*/s32[]{:T(128)}) while((s32[]{:T(128)}, bf16[2,8,128,128]{3,1,0,2:T(8,128)(2,1)S(1)}, bf16[2,8,128,128]{3,2,1,0:T(8,128)(2,1)S(1)}, ...), condition=%wide.region_4.5_spmd, body=%wide.region_0.4_spmd.sunk | while | flops 205259904 | bytes 9355345 | solution.py:70
  39.5 0.2 fusion.125
  39.8 0.4 convolution_convert_fusion.5
  40.2 0.4 copy.88
  40.6 2.2 %fusion.126 = (f32[8,4,128]{2,1,0:T(4,128)S(1)}, f32[8,4,128,128]{2,3,1,0:T(8,128)}) fusion(bf16[8,128,3,4,32]{1,4,3,2,0:T(8,128)(2,1)S(1)} %bitcast.217), kind=kOutput, calls=%fused_computation.134.clone.1 | convolution fusion | flops 35127424 | bytes 2637824 | tf_op jit(solution)/shard_map/while/body/eval_jaxpr/sub | solution.py:52
  42.8 2.0 %convolution_convert_fusion.6 = bf16[8,4,32,128]{3,2,1,0:T(8,128)(2,1)S(1)} fusion(f32[8,4,128,128]{2,3,1,0:T(8,128)} %get-tuple-element.78, f32[8,4,128]{2,1,0:T(4,128)S(1)} %get-tuple-element.79, bf16[8,128,3,4,32]{1,4,3,2,0:T(8,128)(2,1)S(1)} %bitcast.218), kind=kOutput, calls=%fused_computation.7.clone.1 | convolution fusion | flops 34734080 | bytes 2637824 | tf_op jit(solution)/shard_map/while/body/eval_jaxpr/chqk,ckhd->cqhd/dot_general | solution.py:53
  44.8 0.3 fusion.127
  45.1 0.2 copy_dynamic-update-slice_fusion.2
  45.3 0.2 fusion.125
  45.5 0.4 convolution_convert_fusion.5
  46.0 0.4 copy.88
  46.3 2.2 %fusion.126 = (f32[8,4,128]{2,1,0:T(4,128)S(1)}, f32[8,4,128,128]{2,3,1,0:T(8,128)}) fusion(bf16[8,128,3,4,32]{1,4,3,2,0:T(8,128)(2,1)S(1)} %bitcast.217), kind=kOutput, calls=%fused_computation.134.clone.1 | convolution fusion | flops 35127424 | bytes 2637824 | tf_op jit(solution)/shard_map/while/body/eval_jaxpr/sub | solution.py:52
  48.6 2.0 %convolution_convert_fusion.6 = bf16[8,4,32,128]{3,2,1,0:T(8,128)(2,1)S(1)} fusion(f32[8,4,128,128]{2,3,1,0:T(8,128)} %get-tuple-element.78, f32[8,4,128]{2,1,0:T(4,128)S(1)} %get-tuple-element.79, bf16[8,128,3,4,32]{1,4,3,2,0:T(8,128)(2,1)S(1)} %bitcast.218), kind=kOutput, calls=%fused_computation.7.clone.1 | convolution fusion | flops 34734080 | bytes 2637824 | tf_op jit(solution)/shard_map/while/body/eval_jaxpr/chqk,ckhd->cqhd/dot_general | solution.py:53
  50.5 0.3 fusion.127
  50.8 0.2 copy_dynamic-update-slice_fusion.2
  51.1 18.2 %all_to_all.27 = bf16[2,8,128,128]{3,1,0,2:T(8,128)(2,1)S(1)} all-to-all(bf16[2,8,128,128]{3,1,0,2:T(8,128)(2,1)S(1)} %get-tuple-element.32), channel_id=1, replica_groups=mesh['xy'=2,'gz'=16] {'gz'}, dimensions={2} | all-to-all | bytes 1048576 | tf_op jit(solution)/shard_map/all_to_all | solution.py:74
  69.2 0.2 fusion.28
  69.4 1.1 %copy.51 = bf16[2,128,8,128]{3,2,1,0:T(8,128)(2,1)} copy(bf16[2,128,8,128]{3,1,2,0:T(8,128)(2,1)S(1)} %fusion.28) | data formatting | bytes 1048576 | tf_op jit(solution)/shard_map/convert_element_type | solution.py:75
  (14 shorter events, 0.1 us)
Async XLA Ops:
  0.0 5.1 %copy-start = (bf16[2,128,8,128]{3,2,1,0:T(8,128)(2,1)S(1)}, bf16[2,128,8,128]{3,2,1,0:T(8,128)(2,1)}, u32[]{:S(2)}) copy-start(bf16[2,128,8,128]{3,2,1,0:T(8,128)(2,1)} %param.7) | copy-start | bytes 1572868
  0.0 7.5 %copy-start.2 = (bf16[3,3,128,128]{3,2,1,0:T(8,128)(2,1)S(1)}, bf16[3,3,128,128]{3,2,1,0:T(8,128)(2,1)}, u32[]{:S(2)}) copy-start(bf16[3,3,128,128]{3,2,1,0:T(8,128)(2,1)} %param.8) | copy-start | bytes 884740
  1.2 3.9 %collective-permute-start = (bf16[2,128,8,128]{3,1,2,0:T(8,128)(2,1)S(1)}, bf16[2,128,8,128]{3,1,2,0:T(8,128)(2,1)S(1)}, u32[]{:S(2)}, u32[]{:S(2)}) collective-permute-start(bf16[2,128,8,128]{3,1,2,0:T(8,128)(2,1)S(1)} %copy.41), channel_id=1, source_target_pairs={{0,16},{1,17},{2,18},{3,19},{4,20},{5,21},{6,22},{7,23},{8,24},{9,... | collective-permute-start | bytes 1572872 | tf_op jit(solution)/shard_map/ppermute | solution.py:14
  3.6 3.8 %collective-permute-start.1 = (bf16[2,128,8,128]{3,1,2,0:T(8,128)(2,1)S(1)}, bf16[2,128,8,128]{3,1,2,0:T(8,128)(2,1)S(1)}, u32[]{:S(2)}, u32[]{:S(2)}) collective-permute-start(bf16[2,128,8,128]{3,1,2,0:T(8,128)(2,1)S(1)} %copy.41), channel_id=1, source_target_pairs={{16,0},{17,1},{18,2},{19,3},{20,4},{21,5},{22,6},{23,7},{24,8},{25... | collective-permute-start | bytes 1572872 | tf_op jit(solution)/shard_map/ppermute | solution.py:17
  11.0 1.4 %copy-start.3 = (bf16[3,3,128,128]{3,2,1,0:T(8,128)(2,1)S(1)}, bf16[3,3,128,128]{3,2,1,0:T(8,128)(2,1)}, u32[]{:S(2)}) copy-start(bf16[3,3,128,128]{3,2,1,0:T(8,128)(2,1)} %param.9) | copy-start | bytes 884740
  15.1 24.4 %copy-start.1 = (bf16[128,128]{1,0:T(8,128)(2,1)S(1)}, bf16[128,128]{1,0:T(8,128)(2,1)}, u32[]{:S(2)}) copy-start(bf16[128,128]{1,0:T(8,128)(2,1)} %param.11) | copy-start | bytes 98308
  15.1 24.4 %copy-start.4 = (bf16[128,384]{1,0:T(8,128)(2,1)S(1)}, bf16[128,384]{1,0:T(8,128)(2,1)}, u32[]{:S(2)}) copy-start(bf16[128,384]{1,0:T(8,128)(2,1)} %param.10) | copy-start | bytes 294916
  16.3 23.1 %all-to-all-start = ((bf16[2,128,8,128]{3,2,0,1:T(8,128)(2,1)}), bf16[2,128,8,128]{3,2,0,1:T(8,128)(2,1)S(1)}, u32[]{:S(2)}, u32[]{:S(2)}) async-start(bf16[2,128,8,128]{3,2,0,1:T(8,128)(2,1)} %copy.47), calls=%async_computation | async-start | bytes 1048576 | tf_op jit(solution)/shard_map/all_to_all | solution.py:72
where the time goes:
time: 70.9 us; the launch traced here: 70.5 us
  blocking collectives  18.2 us (26%)
  waiting for transfers between devices  17.7 us (25%)
  matrix products  17.3 us (24%)
  starting transfers between devices  11.4 us (16%)
  local copies, waits for them, and re-layouts  5.06 us (7%)
    all_to_all x1, blocking collectives, on_device(): lax.all_to_all(attended, 'gz', split_axis=2, concat_axis=1, tiled=True)  18.2 us
    all_to_all x1, waiting for transfers between devices, on_device(): lax.all_to_all(mixed, 'gz', split_axis=1, concat_axis=2, tiled=True)  15.4 us
    all_to_all x1, starting transfers between devices, on_device(): lax.all_to_all(mixed, 'gz', split_axis=1, concat_axis=2, tiled=True)  7.7 us
    dot_general x18, matrix products, conv_local(): jnp.dot(wider[shift_r:shift_r + count, shift_c:shift_c + cols], weight[sh...  7.52 us
    sub x2, matrix products, attend(): probs = jax.nn.softmax(scores, axis=-1).astype(jnp.bfloat16)  4.45 us
    dot_general x2, matrix products, attend(): jnp.einsum('chqk,ckhd->cqhd', probs, split[:, :, 2], preferred_element_ty...  3.93 us
    ppermute x1, starting transfers between devices, padded_2(): lax.ppermute(lax.slice_in_dim(block, block.shape[dim] - width, None, axis...  2.39 us
    ppermute x1, waiting for transfers between devices, padded_2(): lax.ppermute(lax.slice_in_dim(block, 0, width, axis=dim), axis, backward)  2.13 us
  transfers between devices with their start and end apart: 3, of which 3 were waited for; matrix products, arithmetic and copies ran while one was open for 0% of the time, Pallas kernels for 0%

commit v1 on v0

v1 whole, which is shorter than its diff:
```python
import functools
import math

import jax
import jax.numpy as jnp
from jax import lax
from jax.experimental import pallas as pl
from jax.experimental.pallas import tpu as pltpu
from jax.sharding import PartitionSpec as P

HEADS = 4
CHUNKS = 4
MESH = pl.DeviceIdType.MESH
F32 = jnp.float32
BF16 = jnp.bfloat16


def fill_pairs(wide_ref, weight_ref, ch):
    for out_row in range(2):
        for shift_c in range(3):
            col = (out_row * 3 + shift_c) * ch
            for in_row in range(4):
                shift_r = in_row - out_row
                rows = pl.ds(in_row * ch, ch)
                if 0 <= shift_r < 3:
                    wide_ref[rows, pl.ds(col, ch)] = weight_ref[shift_r, shift_c]
                else:
                    wide_ref[rows, pl.ds(col, ch)] = jnp.zeros((ch, ch), BF16)


def conv_pair(src_ref, row, start, size, wide_ref, ch, sz):
    span = pl.ds(start - 2 * sz, size + 4 * sz)
    rows = jnp.concatenate([src_ref[row + i, span, :] for i in range(4)], axis=-1)
    parts = jnp.dot(rows, wide_ref[...], preferred_element_type=F32)
    outs = []
    for out_row in range(2):
        total = None
        for shift_c in range(3):
            col = (out_row * 3 + shift_c) * ch
            at = 2 * sz + (shift_c - 1) * sz
            part = parts[at : at + size, col : col + ch]
            total = part if total is None else total + part
        outs.append(total)
    return outs


def kernel(
    n, np_, vol, w1, w2, wqkv, wout, out,
    vpad, hpad, mixed, wide1, wide2, recv, att, ret,
    load_sem, halo_send, halo_recv, fwd_send, fwd_recv, own_sem, bwd_send, bwd_recv,
):
    count, flat, ch = mixed.shape
    cells = flat // CHUNKS
    unit = cells // n
    sz = unit // 2
    pad = 2 * sz
    me = lax.axis_index("gz")
    p = lax.axis_index("xy")

    load = pltpu.make_async_copy(vol, vpad.at[pl.ds(2, count), pl.ds(pad, flat)], load_sem)
    load.start()

    barrier = pltpu.get_barrier_semaphore()
    for d in range(1, n):
        pl.semaphore_signal(barrier, inc=1, device_id={"gz": lax.rem(me + d, n)}, device_id_type=MESH)

    @pl.when(p > 0)
    def _():
        pl.semaphore_signal(barrier, inc=1, device_id={"xy": p - 1}, device_id_type=MESH)

    @pl.when(p < np_ - 1)
    def _():
        pl.semaphore_signal(barrier, inc=1, device_id={"xy": p + 1}, device_id_type=MESH)

    edge = jnp.zeros((pad, ch), BF16)
    for row in range(count + 4):
        vpad[row, pl.ds(0, pad), :] = edge
        vpad[row, pl.ds(pad + flat, pad), :] = edge
    for row in range(count + 2):
        hpad[row, pl.ds(0, pad), :] = edge
        hpad[row, pl.ds(pad + flat, pad), :] = edge

    @pl.when(p == 0)
    def _():
        vpad[pl.ds(0, 2), pl.ds(pad, flat), :] = jnp.zeros((2, flat, ch), BF16)

    @pl.when(p == np_ - 1)
    def _():
        vpad[pl.ds(count + 2, 2), pl.ds(pad, flat), :] = jnp.zeros((2, flat, ch), BF16)

    extra = jnp.where(p > 0, 1, 0) + jnp.where(p < np_ - 1, 1, 0)
    pl.semaphore_wait(barrier, n - 1 + extra)

    up = pltpu.make_async_remote_copy(
        src_ref=vol.at[pl.ds(0, 2)], dst_ref=vpad.at[pl.ds(count + 2, 2), pl.ds(pad, flat)],
        send_sem=halo_send.at[0], recv_sem=halo_recv.at[0],
        device_id={"xy": p - 1}, device_id_type=MESH,
    )
    down = pltpu.make_async_remote_copy(
        src_ref=vol.at[pl.ds(count - 2, 2)], dst_ref=vpad.at[pl.ds(0, 2), pl.ds(pad, flat)],
        send_sem=halo_send.at[1], recv_sem=halo_recv.at[1],
        device_id={"xy": p + 1}, device_id_type=MESH,
    )

    @pl.when(p > 0)
    def _():
        up.start()

    @pl.when(p < np_ - 1)
    def _():
        down.start()

    fill_pairs(wide1, w1, ch)
    fill_pairs(wide2, w2, ch)
    load.wait()

    @pl.when(p > 0)
    def _():
        up.wait_send()
        down.wait_recv()

    @pl.when(p < np_ - 1)
    def _():
        down.wait_send()
        up.wait_recv()

    done = 0
    for k in range(CHUNKS):
        upto = min((k + 1) * cells + pad, flat)
        size = upto - done
        for pair in range((count + 2) // 2):
            pieces = conv_pair(vpad, 2 * pair, pad + done, size, wide1, ch, sz)
            for i, first in enumerate(pieces):
                row = 2 * pair + i
                half = 0.5 * first
                value = half + half * jnp.tanh(half)
                if row == 0:
                    value = jnp.where(p > 0, value, 0.0)
                if row == count + 1:
                    value = jnp.where(p < np_ - 1, value, 0.0)
                hpad[row, pl.ds(pad + done, size), :] = value.astype(BF16)
        done = upto
        for pair in range(count // 2):
            pieces = conv_pair(hpad, 2 * pair, pad + k * cells, cells, wide2, ch, sz)
            for i, second in enumerate(pieces):
                row = 2 * pair + i
                base = vpad[row + 2, pl.ds(pad + k * cells, cells), :].astype(F32)
                mixed[row, pl.ds(k * cells, cells), :] = (base + second).astype(BF16)
        for d in range(1, n):
            to = lax.rem(me + d, n)
            start = pl.multiple_of(k * cells + to * unit, unit)
            pltpu.make_async_remote_copy(
                src_ref=mixed.at[:, pl.ds(start, unit)], dst_ref=recv.at[k, me],
                send_sem=fwd_send.at[k], recv_sem=fwd_recv.at[k],
                device_id={"gz": to}, device_id_type=MESH,
            ).start()
        start = pl.multiple_of(k * cells + me * unit, unit)
        pltpu.make_async_copy(mixed.at[:, pl.ds(start, unit)], recv.at[k, me], own_sem.at[k]).start()

    width = ch // HEADS
    lane = lax.broadcasted_iota(jnp.int32, (n * sz, ch), 1) // width
    masks = [jnp.where(lane == h, 1.0, 0.0).astype(BF16) for h in range(HEADS)]
    ones = jnp.concatenate(masks, axis=0)
    factor = math.log2(math.e) / math.sqrt(width)
    depth = n * sz
    for k in range(CHUNKS):
        others = recv.at[k, pl.ds(0, n - 1)]
        pltpu.make_async_copy(others, others, fwd_recv.at[k]).wait()
        pltpu.make_async_copy(recv.at[k, 0], recv.at[k, 0], own_sem.at[k]).wait()
        for r in range(count):
            block = recv[k, :, r].astype(F32).reshape(n, 2, sz, ch)
            x = jnp.concatenate([block[:, j].reshape(depth, ch) for j in range(2)], axis=0)
            inv = lax.rsqrt(jnp.mean(x * x, axis=-1, keepdims=True) + 1e-6)
            qkv = (jnp.dot(x.astype(BF16), wqkv[...], preferred_element_type=F32) * inv).astype(BF16)
            contexts = []
            for j in range(2):
                q = qkv[j * depth : (j + 1) * depth, :ch]
                key = qkv[j * depth : (j + 1) * depth, ch : 2 * ch]
                v = qkv[j * depth : (j + 1) * depth, 2 * ch :]
                keys = jnp.concatenate([key * m for m in masks], axis=0)
                scores = lax.dot_general(q, keys, (((1,), (1,)), ((), ())), preferred_element_type=F32)
                probs = []
                for h in range(HEADS):
                    s = scores[:, h * depth : (h + 1) * depth]
                    top = jnp.max(s, axis=-1, keepdims=True)
                    probs.append(jnp.exp2((s - top) * factor).astype(BF16))
                values = jnp.concatenate([jnp.concatenate([v * m for m in masks], axis=0), ones], axis=1)
                sums = jnp.dot(jnp.concatenate(probs, axis=1), values, preferred_element_type=F32)
                contexts.append((sums[:, :ch] / sums[:, ch:]).astype(BF16))
            a = jnp.dot(jnp.concatenate(contexts, axis=0), wout[...], preferred_element_type=F32)
            a = jnp.stack([a[:depth].reshape(n, sz, ch), a[depth:].reshape(n, sz, ch)], axis=1)
            att[k, :, r] = a.reshape(n, 2 * sz, ch).astype(BF16)
        spot = pl.multiple_of(k * cells + me * unit, unit)
        for d in range(1, n):
            to = lax.rem(me + d, n)
            pltpu.make_async_remote_copy(
                src_ref=att.at[k, to], dst_ref=ret.at[:, pl.ds(spot, unit)],
                send_sem=bwd_send.at[k], recv_sem=bwd_recv.at[k],
                device_id={"gz": to}, device_id_type=MESH,
            ).start()
        pltpu.make_async_copy(att.at[k, me], ret.at[:, pl.ds(spot, unit)], own_sem.at[k]).start()

    for k in range(CHUNKS):
        others = recv.at[k, pl.ds(0, n - 1)]
        pltpu.make_async_copy(others, others, bwd_recv.at[k]).wait()
        pltpu.make_async_copy(recv.at[k, 0], recv.at[k, 0], own_sem.at[k]).wait()
        span = pl.ds(k * cells, cells)
        for r in range(count):
            out[r, span, :] = (mixed[r, span, :].astype(F32) + ret[r, span, :].astype(F32)).astype(BF16)
    for k in range(CHUNKS):
        others = recv.at[k, pl.ds(0, n - 1)]
        pltpu.make_async_copy(others, others, fwd_send.at[k]).wait()
        pltpu.make_async_copy(others, others, bwd_send.at[k]).wait()


def on_device(volume, conv_first, conv_second, w_qkv, w_out):
    count, wide, sz, ch = volume.shape
    n, np_ = lax.axis_size("gz"), lax.axis_size("xy")
    flat = wide * sz
    unit = flat // CHUNKS // n
    vmem = pl.BlockSpec(memory_space=pltpu.VMEM)
    pad = 2 * sz
    out = pl.pallas_call(
        functools.partial(kernel, n, np_),
        out_shape=jax.ShapeDtypeStruct((count, flat, ch), BF16),
        in_specs=[pl.BlockSpec(memory_space=pl.ANY)] + [vmem] * 4,
        out_specs=vmem,
        scratch_shapes=[
            pltpu.VMEM((count + 4, flat + 2 * pad, ch), BF16),
            pltpu.VMEM((count + 2, flat + 2 * pad, ch), BF16),
            pltpu.VMEM((count, flat, ch), BF16),
            pltpu.VMEM((4 * ch, 6 * ch), BF16),
            pltpu.VMEM((4 * ch, 6 * ch), BF16),
            pltpu.VMEM((CHUNKS, n, count, unit, ch), BF16),
            pltpu.VMEM((CHUNKS, n, count, unit, ch), BF16),
            pltpu.VMEM((count, flat, ch), BF16),
            pltpu.SemaphoreType.DMA(()),
            pltpu.SemaphoreType.DMA((2,)),
            pltpu.SemaphoreType.DMA((2,)),
            pltpu.SemaphoreType.DMA((CHUNKS,)),
            pltpu.SemaphoreType.DMA((CHUNKS,)),
            pltpu.SemaphoreType.DMA((CHUNKS,)),
            pltpu.SemaphoreType.DMA((CHUNKS,)),
            pltpu.SemaphoreType.DMA((CHUNKS,)),
        ],
        compiler_params=pltpu.CompilerParams(
            collective_id=0, has_side_effects=True, vmem_limit_bytes=48 * 1024 * 1024
        ),
        cost_estimate=pl.CostEstimate(
            flops=2 * count * flat * ch * ch * 24, bytes_accessed=4 * count * flat * ch, transcendentals=0
        ),
    )(volume.reshape(count, flat, ch), conv_first, conv_second, w_qkv, w_out)
    return out.reshape(volume.shape)


def solution(mesh):
    placed = (P("xy", None, "gz", None), P(), P(), P(), P())
    return jax.shard_map(
        on_device, mesh=mesh, in_specs=placed, out_specs=P("xy", None, "gz", None), check_vma=False
    )
```

time: 70.9 us -> 40.3 us (0.57)
  Pallas kernels: 0 us -> 34.6 us
  blocking collectives: 18.2 us -> 0 us
  waiting for transfers between devices: 17.7 us -> 0 us
  matrix products: 17.3 us -> 0 us
  starting transfers between devices: 11.4 us -> 0 us
    pallas_call x0 -> x1, Pallas kernels: none -> 34.6 us  [on_device(): pl.pallas_call(functools.partial(kernel, n, np_), out_shape=jax.ShapeDtyp...]
    all_to_all x1 -> x0, blocking collectives: 18.2 us -> none  [on_device(): lax.all_to_all(attended, 'gz', split_axis=2, concat_axis=1, tiled=True)]
    all_to_all x1 -> x0, waiting for transfers between devices: 15.4 us -> none  [on_device(): lax.all_to_all(mixed, 'gz', split_axis=1, concat_axis=2, tiled=True)]
    dot_general x24 -> x0, matrix products: 12.9 us -> none  [the longest x18 7.52 us: conv_local(): jnp.dot(wider[shift_r:shift_r + count, shift_c:shift_c + cols], weight[sh...]
    all_to_all x1 -> x0, starting transfers between devices: 7.7 us -> none  [on_device(): lax.all_to_all(mixed, 'gz', split_axis=1, concat_axis=2, tiled=True)]
    sub x2 -> x0, matrix products: 4.45 us -> none  [attend(): probs = jax.nn.softmax(scores, axis=-1).astype(jnp.bfloat16)]
    unnamed x13 -> x11, local copies, waits for them, and re-layouts: 1.4 us -> 5.41 us
    ppermute x2 -> x0, starting transfers between devices: 3.68 us -> none  [the longest x1 2.39 us: padded_2(): lax.ppermute(lax.slice_in_dim(block, block.shape[dim] - width, None, axis...]
  transfers between devices with their start and end apart: 3 -> 0, of which waited for: 3 -> 0; matrix products, arithmetic and copies ran while one was open for 0% -> 0% of each run, Pallas kernels for 0% -> 0%
where the time goes in v1:
time: 40.3 us; the launch traced here: 40 us
  Pallas kernels  34.6 us (86%)
  local copies, waits for them, and re-layouts  5.41 us (13%)
    pallas_call x1, Pallas kernels, on_device(): pl.pallas_call(functools.partial(kernel, n, np_), out_shape=jax.ShapeDtyp...  34.6 us
    unnamed x11, local copies, waits for them, and re-layouts  5.41 us

profile of v1, /device:TPU:0, one launch (start us, length us, event | category | flops | bytes accessed | tf_op | source)
XLA Modules:
  0.0 40.0 jit_solution(18329268649442472938)
XLA Ops:
  0.0 0.0 copy-start
  0.0 1.0 %copy-done = bf16[2,128,8,128]{3,2,1,0:T(8,128)(2,1)S(1)} copy-done((bf16[2,128,8,128]{3,2,1,0:T(8,128)(2,1)S(1)}, bf16[2,128,8,128]{3,2,1,0:T(8,128)(2,1)}, u32[]{:S(2)}) %copy-start) | copy-done | bytes 524312
  1.0 0.0 copy-start.1
  1.0 1.0 %copy-done.1 = bf16[3,3,128,128]{3,2,1,0:T(8,128)(2,1)S(1)} copy-done((bf16[3,3,128,128]{3,2,1,0:T(8,128)(2,1)S(1)}, bf16[3,3,128,128]{3,2,1,0:T(8,128)(2,1)}, u32[]{:S(2)}) %copy-start.1) | copy-done | bytes 294936
  2.0 0.0 copy-start.2
  2.0 1.0 %copy-done.2 = bf16[3,3,128,128]{3,2,1,0:T(8,128)(2,1)S(1)} copy-done((bf16[3,3,128,128]{3,2,1,0:T(8,128)(2,1)S(1)}, bf16[3,3,128,128]{3,2,1,0:T(8,128)(2,1)}, u32[]{:S(2)}) %copy-start.2) | copy-done | bytes 294936
  3.0 0.0 copy-start.3
  3.0 0.9 %copy-done.3 = bf16[128,384]{1,0:T(8,128)(2,1)S(1)} copy-done((bf16[128,384]{1,0:T(8,128)(2,1)S(1)}, bf16[128,384]{1,0:T(8,128)(2,1)}, u32[]{:S(2)}) %copy-start.3) | copy-done | bytes 98328
  3.9 0.0 copy-start.4
  3.9 0.8 %copy-done.4 = bf16[128,128]{1,0:T(8,128)(2,1)S(1)} copy-done((bf16[128,128]{1,0:T(8,128)(2,1)S(1)}, bf16[128,128]{1,0:T(8,128)(2,1)}, u32[]{:S(2)}) %copy-start.4) | copy-done | bytes 32792
  4.6 34.6 %shard_map.55 = bf16[2,1024,128]{2,1,0:T(8,128)(2,1)S(1)} custom-call(bf16[2,1024,128]{2,1,0:T(8,128)(2,1)S(1)} %bitcast.3, bf16[3,3,128,128]{3,2,1,0:T(8,128)(2,1)S(1)} %copy-done.1, bf16[3,3,128,128]{3,2,1,0:T(8,128)(2,1)S(1)} %copy-done.2, bf16[128,384]{1,0:T(8,128)(2,1)S(1)} %copy-done.3, bf16[128,128]{1,0:T(8,128)(2,1)S(1)} %copy-done.4), custom_call_target="tpu_custom_call" | custom-call | flops 1610612736 | bytes 1048576 | tf_op jit(solution)/shard_map/pallas_call | solution.py:223
  39.2 0.8 %copy.7 = bf16[2,128,8,128]{3,2,1,0:T(8,128)(2,1)} copy(bf16[2,128,8,128]{3,2,1,0:T(8,128)(2,1)S(1)} %bitcast.2) | data formatting | bytes 1048576
Async XLA Ops:
  0.0 1.0 %copy-start = (bf16[2,128,8,128]{3,2,1,0:T(8,128)(2,1)S(1)}, bf16[2,128,8,128]{3,2,1,0:T(8,128)(2,1)}, u32[]{:S(2)}) copy-start(bf16[2,128,8,128]{3,2,1,0:T(8,128)(2,1)} %param.5) | copy-start | bytes 1572868
  1.0 1.0 %copy-start.1 = (bf16[3,3,128,128]{3,2,1,0:T(8,128)(2,1)S(1)}, bf16[3,3,128,128]{3,2,1,0:T(8,128)(2,1)}, u32[]{:S(2)}) copy-start(bf16[3,3,128,128]{3,2,1,0:T(8,128)(2,1)} %w1.1) | copy-start | bytes 884740
  2.0 1.0 %copy-start.2 = (bf16[3,3,128,128]{3,2,1,0:T(8,128)(2,1)S(1)}, bf16[3,3,128,128]{3,2,1,0:T(8,128)(2,1)}, u32[]{:S(2)}) copy-start(bf16[3,3,128,128]{3,2,1,0:T(8,128)(2,1)} %w2.1) | copy-start | bytes 884740
  3.0 0.9 %copy-start.3 = (bf16[128,384]{1,0:T(8,128)(2,1)S(1)}, bf16[128,384]{1,0:T(8,128)(2,1)}, u32[]{:S(2)}) copy-start(bf16[128,384]{1,0:T(8,128)(2,1)} %wqkv.1) | copy-start | bytes 294916
  3.9 0.8 %copy-start.4 = (bf16[128,128]{1,0:T(8,128)(2,1)S(1)}, bf16[128,128]{1,0:T(8,128)(2,1)}, u32[]{:S(2)}) copy-start(bf16[128,128]{1,0:T(8,128)(2,1)} %wout.1) | copy-start | bytes 98308

commit v2 on v1

--- a/solution.py
+++ b/solution.py
@@ -45,9 +45,10 @@
 
 
 def kernel(
-    n, np_, vol, w1, w2, wqkv, wout, out,
+    n, np_, vol, w1_in, w2_in, wqkv_in, wout_in, out,
+    w1, w2, wqkv, wout,
     vpad, hpad, mixed, wide1, wide2, recv, att, ret,
-    load_sem, halo_send, halo_recv, fwd_send, fwd_recv, own_sem, bwd_send, bwd_recv,
+    load_sem, weight_sem, halo_send, halo_recv, fwd_send, fwd_recv, own_sem, bwd_send, bwd_recv,
 ):
     count, flat, ch = mixed.shape
     cells = flat // CHUNKS
@@ -59,6 +60,12 @@
 
     load = pltpu.make_async_copy(vol, vpad.at[pl.ds(2, count), pl.ds(pad, flat)], load_sem)
     load.start()
+    weights = [
+        pltpu.make_async_copy(src, dst, weight_sem.at[i])
+        for i, (src, dst) in enumerate(((w1_in, w1), (w2_in, w2), (wqkv_in, wqkv), (wout_in, wout)))
+    ]
+    for copy in weights:
+        copy.start()
 
     barrier = pltpu.get_barrier_semaphore()
     for d in range(1, n):
@@ -110,6 +117,8 @@
     def _():
         down.start()
 
+    for copy in weights:
+        copy.wait()
     fill_pairs(wide1, w1, ch)
     fill_pairs(wide2, w2, ch)
     load.wait()
@@ -223,9 +232,13 @@
     out = pl.pallas_call(
         functools.partial(kernel, n, np_),
         out_shape=jax.ShapeDtypeStruct((count, flat, ch), BF16),
-        in_specs=[pl.BlockSpec(memory_space=pl.ANY)] + [vmem] * 4,
+        in_specs=[pl.BlockSpec(memory_space=pl.ANY)] * 5,
         out_specs=vmem,
         scratch_shapes=[
+            pltpu.VMEM(conv_first.shape, BF16),
+            pltpu.VMEM(conv_second.shape, BF16),
+            pltpu.VMEM(w_qkv.shape, BF16),
+            pltpu.VMEM(w_out.shape, BF16),
             pltpu.VMEM((count + 4, flat + 2 * pad, ch), BF16),
             pltpu.VMEM((count + 2, flat + 2 * pad, ch), BF16),
             pltpu.VMEM((count, flat, ch), BF16),
@@ -235,6 +248,7 @@
             pltpu.VMEM((CHUNKS, n, count, unit, ch), BF16),
             pltpu.VMEM((count, flat, ch), BF16),
             pltpu.SemaphoreType.DMA(()),
+            pltpu.SemaphoreType.DMA((4,)),
             pltpu.SemaphoreType.DMA((2,)),
             pltpu.SemaphoreType.DMA((2,)),
             pltpu.SemaphoreType.DMA((CHUNKS,)),
@@ -244,7 +258,7 @@
             pltpu.SemaphoreType.DMA((CHUNKS,)),
         ],
         compiler_params=pltpu.CompilerParams(
-            collective_id=0, has_side_effects=True, vmem_limit_bytes=48 * 1024 * 1024
+            collective_id=0, has_side_effects=True, vmem_limit_bytes=60 * 1024 * 1024
         ),
         cost_estimate=pl.CostEstimate(
             flops=2 * count * flat * ch * ch * 24, bytes_accessed=4 * count * flat * ch, transcendentals=0

time: 40.3 us -> 37.5 us (0.931)
  local copies, waits for them, and re-layouts: 5.41 us -> 1.87 us
  Pallas kernels: 34.6 us -> 35.5 us
    unnamed x11 -> x1, local copies, waits for them, and re-layouts: 5.41 us -> 1.87 us
    pallas_call x1, Pallas kernels: 34.6 us -> 35.5 us  [on_device(): pl.pallas_call(functools.partial(kernel, n, np_), out_shape=jax.ShapeDtyp...]
where the time goes in v2:
time: 37.5 us; the launch traced here: 37.4 us
  Pallas kernels  35.5 us (95%)
  local copies, waits for them, and re-layouts  1.87 us (5%)
    pallas_call x1, Pallas kernels, on_device(): pl.pallas_call(functools.partial(kernel, n, np_), out_shape=jax.ShapeDtyp...  35.5 us
    unnamed x1, local copies, waits for them, and re-layouts  1.87 us

profile of v2, /device:TPU:0, one launch (start us, length us, event | category | flops | bytes accessed | tf_op | source)
XLA Modules:
  0.0 37.4 jit_solution(8803807054737566293)
XLA Ops:
  0.0 35.5 %shard_map.55 = bf16[2,1024,128]{2,1,0:T(8,128)(2,1)} custom-call(bf16[2,1024,128]{2,1,0:T(8,128)(2,1)} %bitcast.3, bf16[3,3,128,128]{3,2,1,0:T(8,128)(2,1)} %w1_in.1, bf16[3,3,128,128]{3,2,1,0:T(8,128)(2,1)} %w2_in.1, bf16[128,384]{1,0:T(8,128)(2,1)} %wqkv_in.1, bf16[128,128]{1,0:T(8,128)(2,1)} %wout_in.1), custom_call_target="tpu_custom_call" | custom-call | flops 1610612736 | bytes 1048576 | tf_op jit(solution)/shard_map/pallas_call | solution.py:232
  35.5 1.9 %copy.7 = bf16[2,128,8,128]{3,2,1,0:T(8,128)(2,1)} copy(bf16[2,128,8,128]{3,2,1,0:T(8,128)(2,1)} %bitcast.2) | data formatting | bytes 1048576

commit v3 on v2

--- a/solution.py
+++ b/solution.py
@@ -98,24 +98,30 @@
     extra = jnp.where(p > 0, 1, 0) + jnp.where(p < np_ - 1, 1, 0)
     pl.semaphore_wait(barrier, n - 1 + extra)
 
-    up = pltpu.make_async_remote_copy(
-        src_ref=vol.at[pl.ds(0, 2)], dst_ref=vpad.at[pl.ds(count + 2, 2), pl.ds(pad, flat)],
-        send_sem=halo_send.at[0], recv_sem=halo_recv.at[0],
-        device_id={"xy": p - 1}, device_id_type=MESH,
-    )
-    down = pltpu.make_async_remote_copy(
-        src_ref=vol.at[pl.ds(count - 2, 2)], dst_ref=vpad.at[pl.ds(0, 2), pl.ds(pad, flat)],
-        send_sem=halo_send.at[1], recv_sem=halo_recv.at[1],
-        device_id={"xy": p + 1}, device_id_type=MESH,
-    )
+    marks = [0] + [min((k + 1) * cells + 2 * pad, flat) for k in range(CHUNKS)]
+    ups, downs = [], []
+    for k in range(CHUNKS):
+        span, held = pl.ds(marks[k], marks[k + 1] - marks[k]), pl.ds(pad + marks[k], marks[k + 1] - marks[k])
+        ups.append(pltpu.make_async_remote_copy(
+            src_ref=vol.at[pl.ds(0, 2), span], dst_ref=vpad.at[pl.ds(count + 2, 2), held],
+            send_sem=halo_send.at[0, k], recv_sem=halo_recv.at[0, k],
+            device_id={"xy": p - 1}, device_id_type=MESH,
+        ))
+        downs.append(pltpu.make_async_remote_copy(
+            src_ref=vol.at[pl.ds(count - 2, 2), span], dst_ref=vpad.at[pl.ds(0, 2), held],
+            send_sem=halo_send.at[1, k], recv_sem=halo_recv.at[1, k],
+            device_id={"xy": p + 1}, device_id_type=MESH,
+        ))
 
     @pl.when(p > 0)
     def _():
-        up.start()
+        for up in ups:
+            up.start()
 
     @pl.when(p < np_ - 1)
     def _():
-        down.start()
+        for down in downs:
+            down.start()
 
     for copy in weights:
         copy.wait()
@@ -123,18 +129,16 @@
     fill_pairs(wide2, w2, ch)
     load.wait()
 
-    @pl.when(p > 0)
-    def _():
-        up.wait_send()
-        down.wait_recv()
-
-    @pl.when(p < np_ - 1)
-    def _():
-        down.wait_send()
-        up.wait_recv()
-
     done = 0
     for k in range(CHUNKS):
+        @pl.when(p > 0)
+        def _():
+            downs[k].wait_recv()
+
+        @pl.when(p < np_ - 1)
+        def _():
+            ups[k].wait_recv()
+
         upto = min((k + 1) * cells + pad, flat)
         size = upto - done
         for pair in range((count + 2) // 2):
@@ -216,6 +220,16 @@
         span = pl.ds(k * cells, cells)
         for r in range(count):
             out[r, span, :] = (mixed[r, span, :].astype(F32) + ret[r, span, :].astype(F32)).astype(BF16)
+    @pl.when(p > 0)
+    def _():
+        for up in ups:
+            up.wait_send()
+
+    @pl.when(p < np_ - 1)
+    def _():
+        for down in downs:
+            down.wait_send()
+
     for k in range(CHUNKS):
         others = recv.at[k, pl.ds(0, n - 1)]
         pltpu.make_async_copy(others, others, fwd_send.at[k]).wait()
@@ -249,8 +263,8 @@
             pltpu.VMEM((count, flat, ch), BF16),
             pltpu.SemaphoreType.DMA(()),
             pltpu.SemaphoreType.DMA((4,)),
-            pltpu.SemaphoreType.DMA((2,)),
-            pltpu.SemaphoreType.DMA((2,)),
+            pltpu.SemaphoreType.DMA((2, CHUNKS)),
+            pltpu.SemaphoreType.DMA((2, CHUNKS)),
             pltpu.SemaphoreType.DMA((CHUNKS,)),
             pltpu.SemaphoreType.DMA((CHUNKS,)),
             pltpu.SemaphoreType.DMA((CHUNKS,)),

time: 37.5 us -> 35.3 us (0.941)
  Pallas kernels: 35.5 us -> 33.1 us
    pallas_call x1, Pallas kernels: 35.5 us -> 33.1 us  [on_device(): pl.pallas_call(functools.partial(kernel, n, np_), out_shape=jax.ShapeDtyp...]
where the time goes in v3:
time: 35.3 us; the launch traced here: 34.9 us
  Pallas kernels  33.1 us (94%)
  local copies, waits for them, and re-layouts  1.87 us (5%)
    pallas_call x1, Pallas kernels, on_device(): pl.pallas_call(functools.partial(kernel, n, np_), out_shape=jax.ShapeDtyp...  33.1 us
    unnamed x1, local copies, waits for them, and re-layouts  1.87 us

profile of v3, /device:TPU:0, one launch (start us, length us, event | category | flops | bytes accessed | tf_op | source)
XLA Modules:
  0.0 34.9 jit_solution(15231053134397146088)
XLA Ops:
  0.0 33.1 %shard_map.55 = bf16[2,1024,128]{2,1,0:T(8,128)(2,1)} custom-call(bf16[2,1024,128]{2,1,0:T(8,128)(2,1)} %bitcast.3, bf16[3,3,128,128]{3,2,1,0:T(8,128)(2,1)} %w1_in.1, bf16[3,3,128,128]{3,2,1,0:T(8,128)(2,1)} %w2_in.1, bf16[128,384]{1,0:T(8,128)(2,1)} %wqkv_in.1, bf16[128,128]{1,0:T(8,128)(2,1)} %wout_in.1), custom_call_target="tpu_custom_call" | custom-call | flops 1610612736 | bytes 1048576 | tf_op jit(solution)/shard_map/pallas_call | solution.py:246
  33.1 1.9 %copy.7 = bf16[2,128,8,128]{3,2,1,0:T(8,128)(2,1)} copy(bf16[2,128,8,128]{3,2,1,0:T(8,128)(2,1)} %bitcast.2) | data formatting | bytes 1048576

commit v4 on v3

--- a/solution.py
+++ b/solution.py
@@ -45,10 +45,10 @@
 
 
 def kernel(
-    n, np_, vol, w1_in, w2_in, wqkv_in, wout_in, out,
+    n, np_, vol, w1_in, w2_in, wqkv_in, wout_in, mixed_out, ret,
     w1, w2, wqkv, wout,
-    vpad, hpad, mixed, wide1, wide2, recv, att, ret,
-    load_sem, weight_sem, halo_send, halo_recv, fwd_send, fwd_recv, own_sem, bwd_send, bwd_recv,
+    vpad, hpad, mixed, wide1, wide2, recv, att,
+    load_sem, weight_sem, halo_send, halo_recv, fwd_send, fwd_recv, own_sem, bwd_send, bwd_recv, keep_sem,
 ):
     count, flat, ch = mixed.shape
     cells = flat // CHUNKS
@@ -167,6 +167,8 @@
                 send_sem=fwd_send.at[k], recv_sem=fwd_recv.at[k],
                 device_id={"gz": to}, device_id_type=MESH,
             ).start()
+        span = pl.ds(k * cells, cells)
+        pltpu.make_async_copy(mixed.at[:, span], mixed_out.at[:, span], keep_sem.at[k]).start()
         start = pl.multiple_of(k * cells + me * unit, unit)
         pltpu.make_async_copy(mixed.at[:, pl.ds(start, unit)], recv.at[k, me], own_sem.at[k]).start()
 
@@ -218,8 +220,7 @@
         pltpu.make_async_copy(others, others, bwd_recv.at[k]).wait()
         pltpu.make_async_copy(recv.at[k, 0], recv.at[k, 0], own_sem.at[k]).wait()
         span = pl.ds(k * cells, cells)
-        for r in range(count):
-            out[r, span, :] = (mixed[r, span, :].astype(F32) + ret[r, span, :].astype(F32)).astype(BF16)
+        pltpu.make_async_copy(mixed.at[:, span], mixed_out.at[:, span], keep_sem.at[k]).wait()
     @pl.when(p > 0)
     def _():
         for up in ups:
@@ -241,13 +242,12 @@
     n, np_ = lax.axis_size("gz"), lax.axis_size("xy")
     flat = wide * sz
     unit = flat // CHUNKS // n
-    vmem = pl.BlockSpec(memory_space=pltpu.VMEM)
     pad = 2 * sz
-    out = pl.pallas_call(
+    mixed, ret = pl.pallas_call(
         functools.partial(kernel, n, np_),
-        out_shape=jax.ShapeDtypeStruct((count, flat, ch), BF16),
+        out_shape=[jax.ShapeDtypeStruct((count, flat, ch), BF16)] * 2,
         in_specs=[pl.BlockSpec(memory_space=pl.ANY)] * 5,
-        out_specs=vmem,
+        out_specs=[pl.BlockSpec(memory_space=pl.ANY)] * 2,
         scratch_shapes=[
             pltpu.VMEM(conv_first.shape, BF16),
             pltpu.VMEM(conv_second.shape, BF16),
@@ -260,11 +260,11 @@
             pltpu.VMEM((4 * ch, 6 * ch), BF16),
             pltpu.VMEM((CHUNKS, n, count, unit, ch), BF16),
             pltpu.VMEM((CHUNKS, n, count, unit, ch), BF16),
-            pltpu.VMEM((count, flat, ch), BF16),
             pltpu.SemaphoreType.DMA(()),
             pltpu.SemaphoreType.DMA((4,)),
             pltpu.SemaphoreType.DMA((2, CHUNKS)),
             pltpu.SemaphoreType.DMA((2, CHUNKS)),
+            pltpu.SemaphoreType.DMA((CHUNKS,)),
             pltpu.SemaphoreType.DMA((CHUNKS,)),
             pltpu.SemaphoreType.DMA((CHUNKS,)),
             pltpu.SemaphoreType.DMA((CHUNKS,)),
@@ -278,6 +278,7 @@
             flops=2 * count * flat * ch * ch * 24, bytes_accessed=4 * count * flat * ch, transcendentals=0
         ),
     )(volume.reshape(count, flat, ch), conv_first, conv_second, w_qkv, w_out)
+    out = (mixed.astype(F32) + ret.astype(F32)).astype(BF16)
     return out.reshape(volume.shape)
 
 

time: 35.3 us -> 34.9 us (0.989)
  other arithmetic: 0 us -> 2.13 us
  local copies, waits for them, and re-layouts: 1.87 us -> 0 us
  Pallas kernels: 33.1 us -> 32.5 us
    reshape x0 -> x1, other arithmetic: none -> 2.13 us  [on_device(): return out.reshape(volume.shape)]
    unnamed x1 -> x0, local copies, waits for them, and re-layouts: 1.87 us -> none
    pallas_call x1, Pallas kernels: 33.1 us -> 32.5 us  [on_device(): pl.pallas_call(functools.partial(kernel, n, np_), out_shape=[jax.ShapeDty...]
where the time goes in v4:
time: 34.9 us; the launch traced here: 34.7 us
  Pallas kernels  32.5 us (93%)
  other arithmetic  2.13 us (6%)
    pallas_call x1, Pallas kernels, on_device(): pl.pallas_call(functools.partial(kernel, n, np_), out_shape=[jax.ShapeDty...  32.5 us
    reshape x1, other arithmetic, on_device(): return out.reshape(volume.shape)  2.13 us

profile of v4, /device:TPU:0, one launch (start us, length us, event | category | flops | bytes accessed | tf_op | source)
XLA Modules:
  0.0 34.7 jit_solution(17998950116259177973)
XLA Ops:
  0.0 32.5 %shard_map.55 = (bf16[2,1024,128]{2,1,0:T(8,128)(2,1)}, bf16[2,1024,128]{2,1,0:T(8,128)(2,1)}) custom-call(bf16[2,1024,128]{2,1,0:T(8,128)(2,1)} %bitcast.3, bf16[3,3,128,128]{3,2,1,0:T(8,128)(2,1)} %w1_in.1, bf16[3,3,128,128]{3,2,1,0:T(8,128)(2,1)} %w2_in.1, bf16[128,384]{1,0:T(8,128)(2,1)} %wqkv_in.1, bf16[128,128]{1,0:T(8,128)(2,1)} %wout_in.1), custom_call_target="tpu_custom_call" | custom-call | flops 1610612736 | bytes 1048576 | tf_op jit(solution)/shard_map/pallas_call | solution.py:246
  32.5 2.1 %fusion = bf16[2,128,8,128]{3,2,1,0:T(8,128)(2,1)} fusion(bf16[2,1024,128]{2,1,0:T(8,128)(2,1)} %get-tuple-element.8, bf16[2,1024,128]{2,1,0:T(8,128)(2,1)} %get-tuple-element.7), kind=kLoop, calls=%fused_computation.1 | loop fusion | flops 1048576 | bytes 1572864 | tf_op jit(solution)/shard_map/reshape | solution.py:282

commit v5 on v4

--- a/solution.py
+++ b/solution.py
@@ -123,10 +123,8 @@
         for down in downs:
             down.start()
 
-    for copy in weights:
-        copy.wait()
+    weights[0].wait()
     fill_pairs(wide1, w1, ch)
-    fill_pairs(wide2, w2, ch)
     load.wait()
 
     done = 0
@@ -153,6 +151,9 @@
                     value = jnp.where(p < np_ - 1, value, 0.0)
                 hpad[row, pl.ds(pad + done, size), :] = value.astype(BF16)
         done = upto
+        if k == 0:
+            weights[1].wait()
+            fill_pairs(wide2, w2, ch)
         for pair in range(count // 2):
             pieces = conv_pair(hpad, 2 * pair, pad + k * cells, cells, wide2, ch, sz)
             for i, second in enumerate(pieces):
@@ -178,6 +179,8 @@
     ones = jnp.concatenate(masks, axis=0)
     factor = math.log2(math.e) / math.sqrt(width)
     depth = n * sz
+    for copy in weights[2:]:
+        copy.wait()
     for k in range(CHUNKS):
         others = recv.at[k, pl.ds(0, n - 1)]
         pltpu.make_async_copy(others, others, fwd_recv.at[k]).wait()

time: 34.9 us -> 35.1 us (level)
  no operation moved by 1% of the time
where the time goes in v5:
time: 35.1 us; the launch traced here: 34.9 us
  Pallas kernels  32.8 us (93%)
  other arithmetic  2.13 us (6%)
    pallas_call x1, Pallas kernels, on_device(): pl.pallas_call(functools.partial(kernel, n, np_), out_shape=[jax.ShapeDty...  32.8 us
    reshape x1, other arithmetic, on_device(): return out.reshape(volume.shape)  2.13 us

profile of v5, /device:TPU:0, one launch (start us, length us, event | category | flops | bytes accessed | tf_op | source)
XLA Modules:
  0.0 34.9 jit_solution(7504547813872682750)
XLA Ops:
  0.0 32.8 %shard_map.55 = (bf16[2,1024,128]{2,1,0:T(8,128)(2,1)}, bf16[2,1024,128]{2,1,0:T(8,128)(2,1)}) custom-call(bf16[2,1024,128]{2,1,0:T(8,128)(2,1)} %bitcast.3, bf16[3,3,128,128]{3,2,1,0:T(8,128)(2,1)} %w1_in.1, bf16[3,3,128,128]{3,2,1,0:T(8,128)(2,1)} %w2_in.1, bf16[128,384]{1,0:T(8,128)(2,1)} %wqkv_in.1, bf16[128,128]{1,0:T(8,128)(2,1)} %wout_in.1), custom_call_target="tpu_custom_call" | custom-call | flops 1610612736 | bytes 1048576 | tf_op jit(solution)/shard_map/pallas_call | solution.py:249
  32.8 2.1 %fusion = bf16[2,128,8,128]{3,2,1,0:T(8,128)(2,1)} fusion(bf16[2,1024,128]{2,1,0:T(8,128)(2,1)} %get-tuple-element.8, bf16[2,1024,128]{2,1,0:T(8,128)(2,1)} %get-tuple-element.7), kind=kLoop, calls=%fused_computation.1 | loop fusion | flops 1048576 | bytes 1572864 | tf_op jit(solution)/shard_map/reshape | solution.py:285
